TPU v7x, 32 devices: a whole 2x2x4 slice. The times are simulated.
32 devices in a mesh: ctx: 8 (over y, x, core), head: 4 (over z).
Axes of the slice: x: 2, y: 2, z: 4, core: 2. Of those that a mesh axis runs over, the one named last changes fastest.
Arguments:
- queries: bfloat16 [1024, 4096], P('ctx', 'head')
- cache_keys: bfloat16 [8192, 8, 128], P('ctx', 'head')
- cache_values: bfloat16 [8192, 8, 128], P('ctx', 'head'), may hold values from -6 to 6
- shard_len: int32 [8], P('ctx'), may hold values from 256 to 1024, as said below
- out_proj: bfloat16 [4096, 4096], P('head'), may hold values from -0.5 to 0.5
- states: bfloat16 [1024, 4096], P('ctx', 'head'), may hold values from -6 to 6
- adapter_in: bfloat16 [4096, 128], P('head'), may hold values from -0.09375 to 0.09375
- adapter_out: bfloat16 [128, 4096], P(None, 'head'), may hold values from -0.5 to 0.5
Outputs:
- teacher: bfloat16 [1024, 4096], P('ctx', 'head')
- loss: float32 [], replicated
- grad_in: float32 [4096, 128], P('head')
- grad_out: float32 [128, 4096], P(None, 'head')
Inputs may be any that keep to these rules, and one draw needn't show every extreme that they name: `shard_len`: the first block holds 1024 live positions.
All inputs are finite; a program needn't handle non-finite values.
Results may differ from a plain program's by a relative error of at most 0.012.
Values may be sent and summed in bfloat16 or wider, within the bound.
A program may use at most 64 MiB of HBM per device.

v0:
```python
import math

import jax
import jax.numpy as jnp
from jax import lax
from jax.sharding import PartitionSpec as P


def block_partials(qblock, keys, values, valid, scale):
    score = jnp.einsum("rkgd,nkd->rkgn", qblock, keys, preferred_element_type=jnp.float32) * scale
    score = jnp.where(valid, score, jnp.float32(-1e30))
    largest = jnp.max(score, axis=-1)
    prob = jnp.where(valid, jnp.exp(score - largest[..., None]), jnp.float32(0.0)).astype(
        jnp.bfloat16
    )
    total = jnp.sum(prob.astype(jnp.float32), axis=-1)
    accum = jnp.einsum("rkgn,nkd->rkgd", prob, values, preferred_element_type=jnp.float32)
    normed = (accum / total[..., None]).astype(jnp.bfloat16)
    return (largest, total, normed)


def shards(queries, cache_keys, cache_values, shard_len, out_proj, states, adapter_in, adapter_out):
    cache_len, kv_local, head_dim = cache_keys.shape
    group = queries.shape[1] // head_dim // kv_local
    scale = head_dim ** (-0.5)
    own_rows = queries.shape[0]
    whole = lax.all_gather(queries, "ctx", axis=0, tiled=True)
    all_rows = whole.shape[0]
    block = math.gcd(all_rows, 512)
    shaped = whole.reshape(all_rows // block, block, kv_local, group, head_dim)
    valid = jnp.arange(cache_len, dtype=jnp.int32) < shard_len[0]
    largest, total, normed = lax.map(
        lambda qblock: block_partials(qblock, cache_keys, cache_values, valid, scale), shaped
    )
    largest = largest.reshape(all_rows, kv_local, group)
    total = total.reshape(all_rows, kv_local, group)
    normed = normed.reshape(all_rows, kv_local, group, head_dim)
    top = lax.pmax(largest.astype(jnp.bfloat16), "ctx").astype(largest.dtype)
    weight = total * jnp.exp(largest - top)
    sum_acc, sum_tot = (
        lax.psum_scatter(
            normed.astype(jnp.float32) * weight[..., None], "ctx", scatter_dimension=0, tiled=True
        ),
        lax.psum_scatter(weight, "ctx", scatter_dimension=0, tiled=True),
    )
    attn = (sum_acc / sum_tot[..., None]).astype(jnp.bfloat16).reshape(own_rows, -1)
    projected = jnp.dot(attn, out_proj, preferred_element_type=jnp.float32)
    teacher = lax.psum_scatter(projected, "head", scatter_dimension=1, tiled=True).astype(
        jnp.bfloat16
    )
    hidden = lax.psum(jnp.dot(states, adapter_in, preferred_element_type=jnp.float32), "head")
    active = jax.nn.silu(hidden).astype(jnp.bfloat16)
    diff = jnp.dot(active, adapter_out, preferred_element_type=jnp.float32) - teacher.astype(
        jnp.float32
    )
    total_rows = own_rows * lax.axis_size("ctx")
    total_width = states.shape[1] * lax.axis_size("head")
    loss_part = jnp.sum(diff * diff) / (total_rows * total_width)
    cotan = (diff / jnp.sqrt(jnp.float32(total_rows))).astype(jnp.bfloat16)
    grad_out_part = lax.dot_general(
        active, cotan, (((0,), (0,)), ((), ())), preferred_element_type=jnp.float32
    )
    back_part = lax.dot_general(
        cotan, adapter_out, (((1,), (1,)), ((), ())), preferred_element_type=jnp.float32
    )
    sig = jax.nn.sigmoid(hidden)
    back = lax.psum(back_part, "head")
    inner = (back * sig * (1.0 + hidden * (1.0 - sig))).astype(jnp.bfloat16)
    grad_in_part = lax.dot_general(
        states, inner, (((0,), (0,)), ((), ())), preferred_element_type=jnp.float32
    )
    grad_in, grad_out = (
        lax.psum(grad_in_part.astype(jnp.bfloat16), "ctx").astype(jnp.float32),
        lax.psum(grad_out_part.astype(jnp.bfloat16), "ctx").astype(jnp.float32),
    )
    loss = lax.psum(loss_part, ("ctx", "head"))
    return (teacher, loss, grad_in, grad_out)


def solution(mesh):
    placed = (
        P("ctx", "head"),
        P("ctx", "head", None),
        P("ctx", "head", None),
        P("ctx"),
        P("head", None),
        P("ctx", "head"),
        P("head", None),
        P(None, "head"),
    )
    return jax.shard_map(
        shards,
        mesh=mesh,
        in_specs=placed,
        out_specs=(P("ctx", "head"), P(), P("head", None), P(None, "head")),
        check_vma=False,
    )
```

profile of v0, /device:TPU:0, one launch (start us, length us, event | category | flops | bytes accessed | tf_op | source)
XLA Modules:
  0.0 380.1 jit_solution(4929994174807311381)
XLA Ops:
  8.0 1.1 copy.31
  9.1 1.1 copy.32
  10.2 30.3 %all-gather.2.cloned.1.call-done = bf16[1024,1024]{1,0:T(8,128)(2,1)} async-done(((bf16[128,1024]{1,0:T(8,128)(2,1)}), bf16[1024,1024]{1,0:T(8,128)(2,1)}) %all-gather.2.cloned.1.call-update) | async-done | bytes 2097168 | tf_op jit(solution)/shard_map/all_gather | solution.py:27
  40.5 3.2 reshape.27
  43.8 29.0 %while.15 = (s32[]{:T(128)}, f32[2,512,2,4]{1,0,3,2:T(2,128)S(1)}, f32[2,512,2,4]{1,0,3,2:T(2,128)S(1)}, bf16[2,512,2,4,128]{4,1,0,3,2:T(8,128)(2,1)}, bf16[2,51...) while((s32[]{:T(128)}, f32[2,512,2,4]{1,0,3,2:T(2,128)S(1)}, ...), condition=%wide.region_3.4_spmd.clone, body=%wide.region_0.3_spmd.clone.sunk | while | flops 2211439616 | bytes 72570032 | solution.py:32
  44.8 2.7 bitcast_reduce_fusion.2
  47.5 4.6 %convert_reduce_fusion.2 = f32[512,2,4]{0,2,1:T(4,128)S(1)} fusion(f32[512,2,4]{0,2,1:T(4,128)S(1)} %get-tuple-element.191, f32[2,512,4,1024]{3,1,2,0:T(8,128)S(1)} %get-tuple-element.192, pred[1024]{0:T(1024)(128)(4,1)S(1)} %iota_compare_fusion.2), kind=kLoop, calls=%fused_computation.6.clone.1 | loop fusion | flops 29356032 | bytes 16811008 | tf_op jit(solution)/shard_map/while/body/eval_jaxpr/reduce_sum | solution.py:16
  52.2 4.5 %fusion.32 = bf16[2,512,2,4,128]{4,1,0,3,2:T(8,128)(2,1)S(1)} fusion(bf16[2,512,2,4,128]{4,1,0,3,2:T(8,128)(2,1)S(1)} %copy-done.1, s32[]{:T(128)} %get-tuple-element.203, f32[512,2,4]{0,2,1:T(4,128)S(1)} %convert_reduce_fusion.2, bf16[1024,2,128]{2,0,1:T(8,128)(2,1)S(1)} %get-tuple-element.219, f32[2,512,4,1024]{3,1,2,0:T(8,128)S(1)} %get-tuple-element.192, ...), kind=kOutput, calls=%fused_computation.11.clone.1 | convolution fusion | flops 1095761920 | bytes 18384900 | tf_op jit(solution)/shard_map/while/body/eval_jaxpr/rkgn,nkd->rkgd/dot_general | solution.py:17
  56.7 1.3 copy-done.2
  59.3 2.7 bitcast_reduce_fusion.2
  62.0 4.6 %convert_reduce_fusion.2 = f32[512,2,4]{0,2,1:T(4,128)S(1)} fusion(f32[512,2,4]{0,2,1:T(4,128)S(1)} %get-tuple-element.191, f32[2,512,4,1024]{3,1,2,0:T(8,128)S(1)} %get-tuple-element.192, pred[1024]{0:T(1024)(128)(4,1)S(1)} %iota_compare_fusion.2), kind=kLoop, calls=%fused_computation.6.clone.1 | loop fusion | flops 29356032 | bytes 16811008 | tf_op jit(solution)/shard_map/while/body/eval_jaxpr/reduce_sum | solution.py:16
  66.7 4.5 %fusion.32 = bf16[2,512,2,4,128]{4,1,0,3,2:T(8,128)(2,1)S(1)} fusion(bf16[2,512,2,4,128]{4,1,0,3,2:T(8,128)(2,1)S(1)} %copy-done.1, s32[]{:T(128)} %get-tuple-element.203, f32[512,2,4]{0,2,1:T(4,128)S(1)} %convert_reduce_fusion.2, bf16[1024,2,128]{2,0,1:T(8,128)(2,1)S(1)} %get-tuple-element.219, f32[2,512,4,1024]{3,1,2,0:T(8,128)S(1)} %get-tuple-element.192, ...), kind=kOutput, calls=%fused_computation.11.clone.1 | convolution fusion | flops 1095761920 | bytes 18384900 | tf_op jit(solution)/shard_map/while/body/eval_jaxpr/rkgn,nkd->rkgd/dot_general | solution.py:17
  71.2 1.3 copy-done.2
  72.8 23.5 %pmax.7 = bf16[1024,2,4]{0,2,1:T(4,128)(2,1)S(1)} all-reduce(bf16[1024,2,4]{0,2,1:T(4,128)(2,1)S(1)} %convert_element_type.56), channel_id=1, replica_groups=mesh['ctx'=8,'head'=4] {'ctx'}, use_global_device_ids=true, to_apply=%region_4.5 | all-reduce | flops 8192 | bytes 32768 | tf_op jit(solution)/shard_map/pmax | solution.py:38
  96.4 1.0 copy.42
  97.5 3.8 convert_multiply_fusion
  101.4 30.4 %reduce-scatter.10.cloned.1.call-done = f32[128,8]{1,0:T(8,128)} async-done(((f32[1024,8]{1,0:T(8,128)}), f32[128,8]{1,0:T(8,128)}) %reduce-scatter.10.cloned.1.call-update) | async-done | bytes 4112
  131.8 0.9 copy.43
  132.7 54.2 %reduce-scatter.6.cloned.1.call-done = f32[128,2,4,128]{3,0,2,1:T(8,128)} async-done(((f32[1024,2,4,128]{3,0,2,1:T(8,128)}), f32[128,2,4,128]{3,0,2,1:T(8,128)}) %reduce-scatter.6.cloned.1.call-update) | async-done | bytes 524304 | tf_op jit(solution)/shard_map/reduce_scatter | solution.py:41
  186.9 1.2 divide_convert_fusion
  188.3 6.1 %fusion.18 = f32[128,4096]{1,0:T(8,128)} fusion(bf16[128,1024]{0,1:T(8,128)(2,1)S(1)} %bitcast.92, bf16[1024,4096]{1,0:T(8,128)(2,1)} %param.14), kind=kOutput, calls=%fused_computation.35 | convolution fusion | flops 1073741824 | bytes 10747904 | tf_op jit(solution)/shard_map/dot_general | solution.py:47
  195.4 43.0 %reduce-scatter.8.cloned.1.call-done = f32[128,1024]{1,0:T(8,128)} async-done(((f32[128,4096]{1,0:T(8,128)}), f32[128,1024]{1,0:T(8,128)}) %reduce-scatter.8.cloned.1.call-update) | async-done | bytes 524304 | tf_op jit(solution)/shard_map/reduce_scatter | solution.py:48
  238.4 1.1 convert_element_type.59
  239.5 35.1 %all-reduce.5.cloned.1.call-done = f32[128,128]{1,0:T(8,128)} async-done(((f32[128,128]{1,0:T(8,128)}), f32[128,128]{1,0:T(8,128)}) %all-reduce.5.cloned.1.call-update) | async-done | bytes 65552 | tf_op jit(solution)/shard_map/psum | solution.py:51
  274.6 1.7 multiply_reduce_fusion
  277.3 1.8 convolution_convert_fusion
  279.1 32.0 %all-reduce.7.cloned.1.call-done = f32[128,128]{1,0:T(8,128)} async-done(((f32[128,128]{1,0:T(8,128)}), f32[128,128]{1,0:T(8,128)}) %all-reduce.7.cloned.1.call-update) | async-done | bytes 65552 | tf_op jit(solution)/shard_map/psum | solution.py:67
  311.1 1.9 fusion.12
  313.6 40.1 %psum.36 = f32[]{:T(128)} all-reduce(f32[]{:T(128)S(6)} %div.33), channel_id=1, replica_groups=mesh['ctx'=8,'head'=4] {'ctx','head'}, use_global_device_ids=true, to_apply=%region_10.11 | all-reduce | flops 1 | bytes 8 | tf_op jit(solution)/shard_map/psum | solution.py:76
  353.7 15.9 %all-reduce.9.cloned.1.call-done = (bf16[1024,128]{0,1:T(8,128)(2,1)}, bf16[128,1024]{1,0:T(8,128)(2,1)}) async-done(((bf16[1024,128]{0,1:T(8,128)(2,1)}, bf16[128,1024]{1,0:T(8,128)(2,1)}), (bf16[1024,128]{0,1:T(8,128)(2,1)}, bf16[128,1024]{1,0:T(8,128)(2,1)})) %all-reduce.9.cloned.1.call-update) | async-done | bytes 524304 | tf_op jit(solution)/shard_map/psum | solution.py:73
  369.6 1.8 convert_element_type.68
  371.4 1.9 copy.37
  (51 shorter events, 5.6 us)
Async XLA Ops:
  7.2 267.4 %copy-start = (bf16[128,1024]{1,0:T(8,128)(2,1)S(1)}, bf16[128,1024]{1,0:T(8,128)(2,1)}, u32[]{:S(2)}) copy-start(bf16[128,1024]{1,0:T(8,128)(2,1)} %param.17) | copy-start | bytes 786436
  7.2 33.4 %all-gather.2.cloned.1.call-start = ((), (), s32[]{:S(2)}) async-start(), calls=%async_computation.3 | async-start | bytes 2359296 | tf_op jit(solution)/shard_map/all_gather | solution.py:27
  7.9 123.9 %reduce-scatter.10.cloned.1.call-start = ((), (), s32[]{:S(2)}) async-start(), calls=%async_computation.8 | async-start | bytes 589824
  47.5 4.7 %copy-start.1 = (bf16[2,512,2,4,128]{4,1,0,3,2:T(8,128)(2,1)S(1)}, bf16[2,512,2,4,128]{4,1,0,3,2:T(8,128)(2,1)}, u32[]{:S(2)}) copy-start(bf16[2,512,2,4,128]{4,1,0,3,2:T(8,128)(2,1)} %get-tuple-element.206) | copy-start | bytes 6291460 | tf_op jit(solution)/shard_map/while
  56.7 1.3 copy-start.2
  62.0 4.7 %copy-start.1 = (bf16[2,512,2,4,128]{4,1,0,3,2:T(8,128)(2,1)S(1)}, bf16[2,512,2,4,128]{4,1,0,3,2:T(8,128)(2,1)}, u32[]{:S(2)}) copy-start(bf16[2,512,2,4,128]{4,1,0,3,2:T(8,128)(2,1)} %get-tuple-element.206) | copy-start | bytes 6291460 | tf_op jit(solution)/shard_map/while
  71.2 1.3 copy-start.2
  97.5 89.4 %reduce-scatter.6.cloned.1.call-start = ((), (), s32[]{:S(2)}) async-start(), calls=%async_computation.4 | async-start | bytes 4718592 | tf_op jit(solution)/shard_map/reduce_scatter | solution.py:41
  101.3 137.1 %reduce-scatter.8.cloned.1.call-start = ((), (), s32[]{:S(2)}) async-start(), calls=%async_computation.5 | async-start | bytes 2621440 | tf_op jit(solution)/shard_map/reduce_scatter | solution.py:48
  188.3 6.2 %copy-start.3 = (bf16[128,1024]{1,0:T(8,128)(2,1)S(1)}, bf16[128,1024]{1,0:T(8,128)(2,1)}, u32[]{:S(2)}) copy-start(bf16[128,1024]{1,0:T(8,128)(2,1)} %param.15) | copy-start | bytes 786436
  188.3 6.2 %copy-start.5 = (bf16[1024,128]{1,0:T(8,128)(2,1)S(1)}, bf16[1024,128]{1,0:T(8,128)(2,1)}, u32[]{:S(2)}) copy-start(bf16[1024,128]{1,0:T(8,128)(2,1)} %param.16) | copy-start | bytes 786436
  194.4 80.2 %all-reduce.5.cloned.1.call-start = ((), (), s32[]{:S(2)}) async-start(), calls=%async_computation.6 | async-start | bytes 131072 | tf_op jit(solution)/shard_map/psum | solution.py:51
  195.4 115.7 %all-reduce.7.cloned.1.call-start = ((), (), s32[]{:S(2)}) async-start(), calls=%async_computation.7 | async-start | bytes 131072 | tf_op jit(solution)/shard_map/psum | solution.py:67
  239.5 133.8 %copy-start.4 = (bf16[128,1024]{1,0:T(8,128)(2,1)}, bf16[128,1024]{1,0:T(8,128)(2,1)S(1)}, u32[]{:S(2)}) copy-start(bf16[128,1024]{1,0:T(8,128)(2,1)S(1)} %convert_element_type.59) | copy-start | bytes 786436
  277.2 92.4 %all-reduce.9.cloned.1.call-start = ((), (), s32[]{:S(2)}) async-start(), calls=%async_computation.9 | async-start | bytes 1048576 | tf_op jit(solution)/shard_map/psum | solution.py:73
Sparse Core Ops, SparseCore 0:
  9.9 30.5 all-gather.1
  97.6 34.1 reduce-scatter.9
  135.5 51.3 reduce-scatter.5
  194.5 43.8 reduce-scatter.7
  241.2 33.3 all-reduce.4
  277.4 33.6 all-reduce.6
  315.1 54.4 all-reduce.8
where the time goes:
time: 381 us; the launch traced here: 380 us
  waiting for transfers between devices  242 us (64%)
  blocking collectives  63.7 us (17%)
  matrix products  27.6 us (7%)
  other arithmetic  18.5 us (5%)
  between operations  14.9 us (4%)
  local copies, waits for them, and re-layouts  13.3 us (3%)
    reduce_scatter x1, waiting for transfers between devices, shards(): lax.psum_scatter(normed.astype(jnp.float32) * weight[..., None], 'ctx', s...  54.2 us
    reduce_scatter x1, waiting for transfers between devices, shards(): lax.psum_scatter(projected, 'head', scatter_dimension=1, tiled=True)  43 us
    psum x1, blocking collectives, shards(): loss = lax.psum(loss_part, ('ctx', 'head'))  40.1 us
    psum x1, waiting for transfers between devices, shards(): lax.psum(jnp.dot(states, adapter_in, preferred_element_type=jnp.float32),...  35.1 us
    psum x1, waiting for transfers between devices, shards(): back = lax.psum(back_part, 'head')  32 us
    unnamed x8, waiting for transfers between devices  31.2 us
    all_gather x1, waiting for transfers between devices, shards(): whole = lax.all_gather(queries, 'ctx', axis=0, tiled=True)  30.3 us
    pmax x1, blocking collectives, shards(): top = lax.pmax(largest.astype(jnp.bfloat16), 'ctx').astype(largest.dtype)  23.5 us
  transfers between devices with their start and end apart: 7, of which 7 were waited for; matrix products, arithmetic and copies ran while one was open for 3% of the time, Pallas kernels for 0%

commit v1 on v0

v1 whole, which is shorter than its diff:
```python
import functools
import math

import jax
import jax.numpy as jnp
from jax import lax
from jax.experimental import pallas as pl
from jax.experimental.pallas import tpu as pltpu
from jax.sharding import PartitionSpec as P

F32 = jnp.float32
BF16 = jnp.bfloat16
LANES = 128
CHUNK_ROWS = 16


def dot(a, b, dims=((1,), (0,))):
    return lax.dot_general(a, b, (dims, ((), ())), preferred_element_type=F32)


def remote(src, dst, send, recv, **where):
    return pltpu.make_async_remote_copy(
        src_ref=src, dst_ref=dst, send_sem=send, recv_sem=recv, device_id=where,
        device_id_type=pl.DeviceIdType.MESH,
    )


def kernel(
    nctx, nhead, kv, unit, total_rows, total_width,
    q_ref, k_ref, vt_ref, op_hbm, st_ref, ai_ref, ao_ref,
    teacher_ref, loss_ref, gi_ref, go_ref,
    op, qbuf, mine, mine_ml, part, part_ml, sib_a, sib_ml, merged, merged_ml, recv_a, recv_ml,
    attn, z_out, z_in, hbuf, bbuf, st_all, g_all, l_all, gpart, gred, gfull,
    op_sem, q_send, q_fwd, q_recv, p_send, p_recv, m_send, m_recv, z_send, z_recv,
    h_send, h_recv, b_send, b_recv, s_send, s_fwd, s_recv, g_send, g_recv, l_send, l_recv,
    r_send, r_recv, a_send, a_recv,
):
    c = lax.axis_index("ctx")
    z = lax.axis_index("head")
    chips = nctx // 2
    chip = c // 2
    par = c % 2
    sib = c + 1 - 2 * par
    rows, width = q_ref.shape
    heads = width // LANES
    group = heads // kv

    def peer(i):
        other, bit = 0, 1
        while bit < chips:
            other = other + bit * (((chip // bit) % 2 + (i // bit) % 2) % 2)
            bit *= 2
        return 2 * other + par

    barrier = pltpu.get_barrier_semaphore()

    def greet(k, _):
        pl.semaphore_signal(
            barrier, inc=1, device_id={"ctx": (c + k) % nctx}, device_id_type=pl.DeviceIdType.MESH
        )
        return 0

    def greet_head(k, _):
        pl.semaphore_signal(
            barrier, inc=1, device_id={"head": (z + k) % nhead}, device_id_type=pl.DeviceIdType.MESH
        )
        return 0

    load_op = pltpu.make_async_copy(op_hbm, op, op_sem)
    load_op.start()
    lax.fori_loop(1, nctx, greet, 0)
    lax.fori_loop(1, nhead, greet_head, 0)
    pl.semaphore_wait(barrier, nctx + nhead - 2)

    def loop(low, high, f):
        def step(i, _):
            f(i)
            return 0

        lax.fori_loop(low, high, step, 0)

    def q_direct(i):
        return remote(q_ref, qbuf.at[i, 0], q_send.at[i], q_recv.at[i, 0], ctx=peer(i))

    def q_sib():
        return remote(q_ref, qbuf.at[0, 1], q_send.at[0], q_recv.at[0, 1], ctx=sib)

    def q_forward(i):
        return remote(qbuf.at[i, 0], qbuf.at[i, 1], q_fwd.at[i], q_recv.at[i, 1], ctx=sib)

    q_sib().start()
    loop(1, chips, lambda i: q_direct(i).start())

    def h_copy(k):
        return remote(hbuf.at[z], hbuf.at[z], h_send.at[k], h_recv.at[k], head=(z + k) % nhead)

    def h_in(k):
        return remote(
            hbuf.at[(z - k + nhead) % nhead], hbuf.at[(z - k + nhead) % nhead],
            h_send.at[k], h_recv.at[k], head=(z + k) % nhead,
        )

    hbuf[z] = dot(st_ref[...], ai_ref[...])
    loop(1, nhead, lambda k: h_copy(k).start())

    qbuf[0, 0] = q_ref[...]
    own_rows = pl.ds(pl.multiple_of(c * rows, rows), rows)
    st_all[own_rows, :] = st_ref[...]

    one_hot = jnp.where(
        lax.broadcasted_iota(jnp.int32, (2 * rows, LANES), 1) == 0, 1.0, 0.0
    ).astype(BF16)

    def attend(i, j, out, out_ml):
        for n in range(kv):
            keys = k_ref[n]
            vals = vt_ref[n]
            for g in range(0, group, 2):
                h = n * group + g
                pair = jnp.concatenate(
                    [
                        qbuf[i, j, :, h * LANES : (h + 1) * LANES],
                        qbuf[i, j, :, (h + 1) * LANES : (h + 2) * LANES],
                    ],
                    axis=0,
                )
                score = dot(keys, jnp.concatenate([pair, one_hot], axis=1), ((1,), (1,)))
                top = jnp.max(score, axis=0, keepdims=True)
                prob = jnp.exp2((score - top) * unit).astype(BF16)
                acc = dot(vals, prob)
                tot = acc[LANES : LANES + 1, :]
                norm = (acc[:LANES, :] / tot).astype(BF16)
                for e in range(2):
                    cut = slice(e * rows, (e + 1) * rows)
                    out[i, (h + e) * LANES : (h + e + 1) * LANES, :] = norm[:, cut]
                    out_ml[i, 0, h + e : h + e + 1, :] = top[:, cut]
                    out_ml[i, 1, h + e : h + e + 1, :] = tot[:, cut]

    def p_copy(i):
        return (
            remote(part.at[i], sib_a.at[i], p_send.at[i, 0], p_recv.at[i, 0], ctx=sib),
            remote(part_ml.at[i], sib_ml.at[i], p_send.at[i, 1], p_recv.at[i, 1], ctx=sib),
        )

    def m_copy(i):
        return (
            remote(merged.at[i], recv_a.at[i], m_send.at[i, 0], m_recv.at[i, 0], ctx=peer(i)),
            remote(merged_ml.at[i], recv_ml.at[i], m_send.at[i, 1], m_recv.at[i, 1], ctx=peer(i)),
        )

    def merge(i):
        for copy in p_copy(i):
            copy.wait_recv()
        m0, l0 = mine_ml[i, 0, :heads, :], mine_ml[i, 1, :heads, :]
        m1, l1 = sib_ml[i, 0, :heads, :], sib_ml[i, 1, :heads, :]
        top = jnp.maximum(m0, m1)
        w0 = l0 * jnp.exp2((m0 - top) * unit)
        w1 = l1 * jnp.exp2((m1 - top) * unit)
        tot = w0 + w1
        merged_ml[i, 0, :heads, :] = top
        merged_ml[i, 1, :heads, :] = tot
        f0, f1 = w0 / tot, w1 / tot
        for h in range(heads):
            cut = slice(h * LANES, (h + 1) * LANES)
            merged[i, cut, :] = (
                mine[i, cut, :].astype(F32) * f0[h : h + 1, :]
                + sib_a[i, cut, :].astype(F32) * f1[h : h + 1, :]
            ).astype(BF16)

        @pl.when(i > 0)
        def _():
            for copy in m_copy(i):
                copy.start()

    def chip_step(i):
        @pl.when(i > 0)
        def _():
            q_direct(i).wait_recv()
            q_forward(i).start()

        attend(i, 0, mine, mine_ml)
        q_forward(i).wait_recv()
        attend(i, 1, part, part_ml)
        for copy in p_copy(i):
            copy.start()

        @pl.when(i > 0)
        def _():
            merge(i - 1)

    loop(0, chips, chip_step)
    merge(chips - 1)

    loop(1, nhead, lambda k: h_in(k).wait_recv())
    hidden = hbuf[0]
    for k in range(1, nhead):
        hidden = hidden + hbuf[k]
    sig = jax.nn.sigmoid(hidden)
    active32 = (hidden * sig).astype(BF16).astype(F32)
    active = active32.astype(BF16)
    active_t = active32.T.astype(BF16)

    def wait_partials(i):
        for copy in m_copy(i):
            copy.wait_recv()

    loop(1, chips, wait_partials)

    def s_direct(i):
        return remote(st_ref, st_all.at[own_rows], s_send.at[i], s_recv.at[i, 0], ctx=peer(i))

    def s_sib():
        return remote(st_ref, st_all.at[own_rows], s_send.at[0], s_recv.at[0, 1], ctx=sib)

    def s_forward(i):
        its = pl.ds(pl.multiple_of(peer(i) * rows, rows), rows)
        return remote(st_all.at[its], st_all.at[its], s_fwd.at[i], s_recv.at[i, 1], ctx=sib)

    def s_in(i):
        its = pl.ds(pl.multiple_of(peer(i) * rows, rows), rows)
        return remote(st_ref, st_all.at[its], s_send.at[i], s_recv.at[i, 0], ctx=peer(i))

    def s_in_sib(i):
        owner = peer(i) + 1 - 2 * par
        its = pl.ds(pl.multiple_of(owner * rows, rows), rows)
        return remote(st_ref, st_all.at[its], s_send.at[i], s_recv.at[i, 1], ctx=sib)

    s_sib().start()
    loop(1, chips, lambda i: s_direct(i).start())

    tops = [merged_ml[0, 0, :heads, :]] + [recv_ml[i, 0, :heads, :] for i in range(1, chips)]
    tots = [merged_ml[0, 1, :heads, :]] + [recv_ml[i, 1, :heads, :] for i in range(1, chips)]
    top = functools.reduce(jnp.maximum, tops)
    weights = [t * jnp.exp2((m - top) * unit) for m, t in zip(tops, tots)]
    whole = functools.reduce(jnp.add, weights)
    weights = [w / whole for w in weights]
    for h in range(heads):
        cut = slice(h * LANES, (h + 1) * LANES)
        acc = merged[0, cut, :].astype(F32) * weights[0][h : h + 1, :]
        for i in range(1, chips):
            acc = acc + recv_a[i, cut, :].astype(F32) * weights[i][h : h + 1, :]
        attn[:, cut] = acc.T.astype(BF16)

    load_op.wait()

    def z_copy(k):
        return remote(z_out.at[k], z_in.at[k], z_send.at[k], z_recv.at[k], head=(z + k) % nhead)

    def project(owner):
        cols = pl.ds(pl.multiple_of(owner * width, width), width)
        return dot(attn[...], op[:, cols])

    def z_step(k):
        z_out[k] = project((z + k) % nhead).astype(BF16)
        z_copy(k).start()

    loop(1, nhead, z_step)
    own = project(z)
    student = dot(active, ao_ref[...])

    def s_relay(i):
        s_in(i).wait_recv()
        s_forward(i).start()

    loop(1, chips, s_relay)
    loop(1, nhead, lambda k: z_copy(k).wait_recv())
    for k in range(1, nhead):
        own = own + z_in[k].astype(F32)
    teacher = own.astype(BF16)
    teacher_ref[...] = teacher
    diff = student - teacher.astype(F32)
    cotan = (diff * (1.0 / math.sqrt(total_rows))).astype(BF16)

    bbuf[z, :rows, :] = dot(cotan, ao_ref[...], ((1,), (1,)))
    square = diff * diff
    lane = square[:, :LANES]
    for n in range(1, width // LANES):
        lane = lane + square[:, n * LANES : (n + 1) * LANES]
    bbuf[z, rows : rows + 8, :] = jnp.sum(lane.reshape(rows // 8, 8, LANES), axis=0)

    def b_copy(k):
        return remote(bbuf.at[z], bbuf.at[z], b_send.at[k], b_recv.at[k], head=(z + k) % nhead)

    def b_in(k):
        src = (z - k + nhead) % nhead
        return remote(bbuf.at[src], bbuf.at[src], b_send.at[k], b_recv.at[k], head=(z + k) % nhead)

    loop(1, nhead, lambda k: b_copy(k).start())

    cw = width * (gpart.shape[0] // CHUNK_ROWS) // nctx
    ncol = width // cw

    def chunk(ref, d):
        return ref.at[
            pl.ds(pl.multiple_of((d // ncol) * CHUNK_ROWS, CHUNK_ROWS), CHUNK_ROWS),
            pl.ds(pl.multiple_of((d % ncol) * cw, cw), cw),
        ]

    gpart[...] = dot(active_t, cotan).astype(BF16)

    def r_copy(k):
        d = (c + k) % nctx
        return remote(chunk(gpart, d), gred.at[c], r_send.at[k], r_recv.at[k], ctx=d)

    def r_in(k):
        src = (c - k + nctx) % nctx
        return remote(chunk(gpart, c), gred.at[src], r_send.at[k], r_recv.at[k], ctx=src)

    loop(1, nctx, lambda k: r_copy(k).start())
    gred[c] = chunk(gpart, c)[...]

    loop(1, nhead, lambda k: b_in(k).wait_recv())
    back = bbuf[0]
    for k in range(1, nhead):
        back = back + bbuf[k]
    g_all[own_rows, :] = (
        back[:rows] * sig * (1.0 + hidden * (1.0 - sig))
    ).astype(BF16)
    l_all[c] = back[rows : rows + 8]

    def g_copy(k):
        d = (c + k) % nctx
        return (
            remote(g_all.at[own_rows], g_all.at[own_rows], g_send.at[k], g_recv.at[k], ctx=d),
            remote(l_all.at[c], l_all.at[c], l_send.at[k], l_recv.at[k], ctx=d),
        )

    def g_in(k):
        src = (c - k + nctx) % nctx
        its = pl.ds(pl.multiple_of(src * rows, rows), rows)
        return (
            remote(g_all.at[its], g_all.at[its], g_send.at[k], g_recv.at[k], ctx=src),
            remote(l_all.at[src], l_all.at[src], l_send.at[k], l_recv.at[k], ctx=src),
        )

    def g_start(k):
        for copy in g_copy(k):
            copy.start()

    loop(1, nctx, g_start)

    loop(1, nctx, lambda k: r_in(k).wait_recv())
    total = gred[0].astype(F32)
    for k in range(1, nctx):
        total = total + gred[k].astype(F32)
    chunk(gfull, c)[...] = total.astype(BF16)

    def a_copy(k):
        d = (c + k) % nctx
        return remote(chunk(gfull, c), chunk(gfull, c), a_send.at[k], a_recv.at[k], ctx=d)

    def a_in(k):
        src = (c - k + nctx) % nctx
        return remote(chunk(gfull, src), chunk(gfull, src), a_send.at[k], a_recv.at[k], ctx=src)

    loop(1, nctx, lambda k: a_copy(k).start())

    loop(0, chips, lambda i: s_in_sib(i).wait_recv())

    def g_wait(k):
        for copy in g_in(k):
            copy.wait_recv()

    loop(1, nctx, g_wait)
    inner_t = g_all[...].astype(F32).T.astype(BF16)
    gi_ref[...] = dot(inner_t, st_all[...]).T
    squares = l_all[0]
    for k in range(1, nctx):
        squares = squares + l_all[k]
    loss = jnp.sum(jnp.sum(squares, axis=0, keepdims=True), axis=1, keepdims=True)
    loss_ref[...] = loss / (total_rows * total_width)

    loop(1, nctx, lambda k: a_in(k).wait_recv())
    go_ref[...] = gfull[...].astype(F32)

    q_sib().wait_send()
    s_sib().wait_send()
    p_wait = lambda i: [copy.wait_send() for copy in p_copy(i)] and None
    loop(0, chips, p_wait)

    def chips_sent(i):
        q_direct(i).wait_send()
        q_forward(i).wait_send()
        s_direct(i).wait_send()
        s_forward(i).wait_send()
        for copy in m_copy(i):
            copy.wait_send()

    loop(1, chips, chips_sent)

    def head_sent(k):
        h_copy(k).wait_send()
        z_copy(k).wait_send()
        b_copy(k).wait_send()

    loop(1, nhead, head_sent)

    def ctx_sent(k):
        r_copy(k).wait_send()
        a_copy(k).wait_send()
        for copy in g_copy(k):
            copy.wait_send()

    loop(1, nctx, ctx_sent)


def shards(queries, cache_keys, cache_values, shard_len, out_proj, states, adapter_in, adapter_out):
    nctx, nhead = lax.axis_size("ctx"), lax.axis_size("head")
    rows, width = queries.shape
    length, kv, hd = cache_keys.shape
    rank = adapter_in.shape[1]
    chips = nctx // 2
    unit = hd ** (-0.5) * math.log2(math.e)
    live = jnp.arange(length, dtype=jnp.int32) < shard_len[0]
    bias = jnp.where(live, 0.0, -1e30).astype(BF16)
    first = jnp.arange(hd) == 0
    keys = jnp.transpose(cache_keys, (1, 0, 2))
    extra = jnp.where(first[None, :], bias[:, None], jnp.zeros((), BF16))
    keys = jnp.concatenate([keys, jnp.broadcast_to(extra[None], keys.shape)], axis=2)
    vals = jnp.transpose(cache_values, (1, 2, 0))
    vals = jnp.concatenate([vals, jnp.ones((kv, CHUNK_ROWS, length), BF16)], axis=1)
    hpad = -(-(width // LANES) // 8) * 8
    dma = pltpu.SemaphoreType.DMA
    vmem = pl.BlockSpec(memory_space=pltpu.VMEM)
    cw = width * (rank // CHUNK_ROWS) // nctx
    scratch = [
        pltpu.VMEM(out_proj.shape, BF16),
        pltpu.VMEM((chips, 2, rows, width), BF16),
        pltpu.VMEM((chips, width, rows), BF16),
        pltpu.VMEM((chips, 2, hpad, rows), F32),
        pltpu.VMEM((chips, width, rows), BF16),
        pltpu.VMEM((chips, 2, hpad, rows), F32),
        pltpu.VMEM((chips, width, rows), BF16),
        pltpu.VMEM((chips, 2, hpad, rows), F32),
        pltpu.VMEM((chips, width, rows), BF16),
        pltpu.VMEM((chips, 2, hpad, rows), F32),
        pltpu.VMEM((chips, width, rows), BF16),
        pltpu.VMEM((chips, 2, hpad, rows), F32),
        pltpu.VMEM((rows, width), BF16),
        pltpu.VMEM((nhead, rows, width), BF16),
        pltpu.VMEM((nhead, rows, width), BF16),
        pltpu.VMEM((nhead, rows, rank), F32),
        pltpu.VMEM((nhead, rows + 8, rank), F32),
        pltpu.VMEM((nctx * rows, width), BF16),
        pltpu.VMEM((nctx * rows, rank), BF16),
        pltpu.VMEM((nctx, 8, LANES), F32),
        pltpu.VMEM((rank, width), BF16),
        pltpu.VMEM((nctx, CHUNK_ROWS, cw), BF16),
        pltpu.VMEM((rank, width), BF16),
        dma,
        dma((chips,)), dma((chips,)), dma((chips, 2)),
        dma((chips, 2)), dma((chips, 2)),
        dma((chips, 2)), dma((chips, 2)),
        dma((nhead,)), dma((nhead,)),
        dma((nhead,)), dma((nhead,)),
        dma((nhead,)), dma((nhead,)),
        dma((chips,)), dma((chips,)), dma((chips, 2)),
        dma((nctx,)), dma((nctx,)), dma((nctx,)), dma((nctx,)),
        dma((nctx,)), dma((nctx,)), dma((nctx,)), dma((nctx,)),
    ]
    teacher, loss, grad_in, grad_out = pl.pallas_call(
        functools.partial(
            kernel, nctx, nhead, kv, unit, rows * nctx, width * nhead
        ),
        out_shape=(
            jax.ShapeDtypeStruct((rows, width), BF16),
            jax.ShapeDtypeStruct((1, 1), F32),
            jax.ShapeDtypeStruct((width, rank), F32),
            jax.ShapeDtypeStruct((rank, width), F32),
        ),
        in_specs=[vmem, vmem, vmem, pl.BlockSpec(memory_space=pl.ANY), vmem, vmem, vmem],
        out_specs=(vmem, vmem, vmem, vmem),
        scratch_shapes=scratch,
        compiler_params=pltpu.CompilerParams(
            collective_id=0, has_side_effects=True, vmem_limit_bytes=50 * 2**20
        ),
    )(queries, keys, vals, out_proj, states, adapter_in, adapter_out)
    return (teacher, loss.reshape(()), grad_in, grad_out)


def solution(mesh):
    placed = (
        P("ctx", "head"),
        P("ctx", "head", None),
        P("ctx", "head", None),
        P("ctx"),
        P("head", None),
        P("ctx", "head"),
        P("head", None),
        P(None, "head"),
    )
    return jax.shard_map(
        shards,
        mesh=mesh,
        in_specs=placed,
        out_specs=(P("ctx", "head"), P(), P("head", None), P(None, "head")),
        check_vma=False,
    )
```

time: 381 us -> 92 us (0.24)
  waiting for transfers between devices: 242 us -> 0 us
  Pallas kernels: 0 us -> 83.9 us
  blocking collectives: 63.7 us -> 0 us
  matrix products: 27.6 us -> 0 us
  other arithmetic: 18.5 us -> 0.33 us
  between operations: 14.9 us -> 3.08 us
  local copies, waits for them, and re-layouts: 13.3 us -> 4.46 us
    reduce_scatter x2 -> x0, waiting for transfers between devices: 97.2 us -> none  [the longest x1 54.2 us: shards(): lax.psum_scatter(normed.astype(jnp.float32) * weight[..., None], 'ctx', s...]
    pallas_call x0 -> x1, Pallas kernels: none -> 83.9 us  [shards(): pl.pallas_call(functools.partial(kernel, nctx, nhead, kv, unit, rows * nc...]
    psum x3 -> x0, waiting for transfers between devices: 83 us -> none  [the longest x1 35.1 us: shards(): lax.psum(jnp.dot(states, adapter_in, preferred_element_type=jnp.float32),...]
    psum x1 -> x0, blocking collectives: 40.1 us -> none  [shards(): loss = lax.psum(loss_part, ('ctx', 'head'))]
    unnamed x8 -> x0, waiting for transfers between devices: 31.2 us -> none
    all_gather x1 -> x0, waiting for transfers between devices: 30.3 us -> none  [shards(): whole = lax.all_gather(queries, 'ctx', axis=0, tiled=True)]
    dot_general x10 -> x0, matrix products: 27.6 us -> none  [the longest x2 9.05 us: block_partials(): jnp.einsum('rkgn,nkd->rkgd', prob, values, preferred_element_type=jnp.flo...]
    pmax x1 -> x0, blocking collectives: 23.5 us -> none  [shards(): top = lax.pmax(largest.astype(jnp.bfloat16), 'ctx').astype(largest.dtype)]
  transfers between devices with their start and end apart: 7 -> 0, of which waited for: 7 -> 0; matrix products, arithmetic and copies ran while one was open for 3% -> 0% of each run, Pallas kernels for 0% -> 0%
where the time goes in v1:
time: 92 us; the launch traced here: 91.8 us
  Pallas kernels  83.9 us (91%)
  local copies, waits for them, and re-layouts  4.46 us (5%)
  between operations  3.08 us (3%)
    pallas_call x1, Pallas kernels, shards(): pl.pallas_call(functools.partial(kernel, nctx, nhead, kv, unit, rows * nc...  83.9 us
    unnamed x15, local copies, waits for them, and re-layouts  4.38 us

profile of v1, /device:TPU:0, one launch (start us, length us, event | category | flops | bytes accessed | tf_op | source)
XLA Modules:
  0.0 91.8 jit_solution(16458289075579611826)
XLA Ops:
  1.3 0.0 copy-start.4
  1.3 0.2 broadcast_select_fusion
  1.6 1.1 %copy.15 = bf16[1024,2,128]{2,0,1:T(8,128)(2,1)S(1)} copy(bf16[1024,2,128]{2,1,0:T(2,128)(2,1)} %param.9) | data formatting | bytes 1048576 | tf_op args[1]
  2.7 0.0 copy-start
  2.7 0.0 copy-start.1
  2.7 0.0 copy-start.2
  2.7 0.0 copy-start.3
  2.7 0.1 pad_maximum_fusion.k_ref
  2.9 0.0 copy-done.4
  2.9 0.4 copy.13
  3.3 0.3 copy-done
  3.6 0.1 copy-done.1
  3.7 0.1 copy-done.2
  3.8 0.1 copy-done.3
  3.9 83.9 %shard_map.111 = (bf16[128,1024]{1,0:T(8,128)(2,1)S(1)}, f32[1,1]{1,0:T(1,128)}, f32[1024,128]{1,0:T(8,128)S(1)}, f32[128,1024]{1,0:T(8,128)S(1)}) custom-call(bf16[128,1024]{1,0:T(8,128)(2,1)S(1)} %copy-done, bf16[2,1024,256]{2,1,0:T(8,128)(2,1)S(1)} %pad_maximum_fusion.k_ref, bf16[2,144,1024]{2,1,0:T(8,128)(2,1)S(1)} %concatenate.7.vt_ref, ...), custom_call_target="tpu_custom_call" | custom-call | tf_op jit(solution)/shard_map/pallas_call | solution.py:461
  87.8 0.7 copy.21
  89.1 0.8 copy.23
  89.9 0.8 copy.24
  (4 shorter events, 0.1 us)
Async XLA Ops:
  1.3 1.6 %copy-start.4 = (bf16[1024,2,128]{2,1,0:T(2,128)(2,1)S(1)}, bf16[1024,2,128]{2,1,0:T(2,128)(2,1)}, u32[]{:S(2)}) copy-start(bf16[1024,2,128]{2,1,0:T(2,128)(2,1)} %param.10) | copy-start | bytes 1572868
  2.7 1.0 %copy-start = (bf16[128,1024]{1,0:T(8,128)(2,1)S(1)}, bf16[128,1024]{1,0:T(8,128)(2,1)}, u32[]{:S(2)}) copy-start(bf16[128,1024]{1,0:T(8,128)(2,1)} %q_ref.1) | copy-start | bytes 786436
  2.7 1.0 %copy-start.1 = (bf16[128,1024]{1,0:T(8,128)(2,1)S(1)}, bf16[128,1024]{1,0:T(8,128)(2,1)}, u32[]{:S(2)}) copy-start(bf16[128,1024]{1,0:T(8,128)(2,1)} %st_ref.1) | copy-start | bytes 786436
  2.7 1.1 %copy-start.2 = (bf16[1024,128]{1,0:T(8,128)(2,1)S(1)}, bf16[1024,128]{1,0:T(8,128)(2,1)}, u32[]{:S(2)}) copy-start(bf16[1024,128]{1,0:T(8,128)(2,1)} %ai_ref.1) | copy-start | bytes 786436
  2.7 1.2 %copy-start.3 = (bf16[128,1024]{1,0:T(8,128)(2,1)S(1)}, bf16[128,1024]{1,0:T(8,128)(2,1)}, u32[]{:S(2)}) copy-start(bf16[128,1024]{1,0:T(8,128)(2,1)} %ao_ref.1) | copy-start | bytes 786436

commit v2 on v1

v2 whole, which is shorter than its diff:
```python
import functools
import math

import jax
import jax.numpy as jnp
from jax import lax
from jax.experimental import pallas as pl
from jax.experimental.pallas import tpu as pltpu
from jax.sharding import PartitionSpec as P

F32 = jnp.float32
BF16 = jnp.bfloat16
LANES = 128
CHUNK_ROWS = 16


def dot(a, b, dims=((1,), (0,))):
    return lax.dot_general(a, b, (dims, ((), ())), preferred_element_type=F32)


def remote(src, dst, send, recv, **where):
    return pltpu.make_async_remote_copy(
        src_ref=src, dst_ref=dst, send_sem=send, recv_sem=recv, device_id=where,
        device_id_type=pl.DeviceIdType.MESH,
    )


def kernel(
    nctx, nhead, kv, unit, total_rows, total_width,
    q_ref, k_ref, vt_ref, op_hbm, st_ref, ai_ref, ao_ref,
    teacher_ref, loss_ref, gi_ref, go_ref,
    op, qbuf, mine, mine_ml, part, part_ml, sib_a, sib_ml, merged, merged_ml, recv_a, recv_ml,
    attn, own_z, z_out, z_in, hbuf, bbuf, lbuf, st_all, g_all, l_all, gpart, gred, gfull,
    op_sem, q_send, q_fwd, q_recv, p_send, p_recv, m_send, m_recv, z_send, z_recv,
    h_send, h_recv, b_send, b_recv, s_send, s_fwd, s_recv, g_send, g_recv, l_send, l_recv,
    r_send, r_recv, a_send, a_recv,
):
    c = lax.axis_index("ctx")
    z = lax.axis_index("head")
    chips = nctx // 2
    chip = c // 2
    par = c % 2
    sib = c + 1 - 2 * par
    rows, width = q_ref.shape
    heads = width // LANES
    group = heads // kv

    def peer(i):
        other, bit = 0, 1
        while bit < chips:
            other = other + bit * (((chip // bit) % 2 + (i // bit) % 2) % 2)
            bit *= 2
        return 2 * other + par

    barrier = pltpu.get_barrier_semaphore()

    def greet(k, _):
        pl.semaphore_signal(
            barrier, inc=1, device_id={"ctx": (c + k) % nctx}, device_id_type=pl.DeviceIdType.MESH
        )
        return 0

    def greet_head(k, _):
        pl.semaphore_signal(
            barrier, inc=1, device_id={"head": (z + k) % nhead}, device_id_type=pl.DeviceIdType.MESH
        )
        return 0

    load_op = pltpu.make_async_copy(op_hbm, op, op_sem)
    load_op.start()
    lax.fori_loop(1, nctx, greet, 0)
    lax.fori_loop(1, nhead, greet_head, 0)
    pl.semaphore_wait(barrier, nctx + nhead - 2)

    def loop(low, high, f):
        def step(i, _):
            f(i)
            return 0

        lax.fori_loop(low, high, step, 0)

    hrows = rows // 2
    wide = group * hrows

    def half(a):
        return pl.ds(a * hrows, hrows)

    def q_direct(a, i):
        return remote(
            q_ref.at[half(a)], qbuf.at[a, i, 0], q_send.at[a, i], q_recv.at[a, i, 0], ctx=peer(i)
        )

    def q_sib(a):
        return remote(
            q_ref.at[half(a)], qbuf.at[a, 0, 1], q_send.at[a, 0], q_recv.at[a, 0, 1], ctx=sib
        )

    def q_forward(a, i):
        return remote(
            qbuf.at[a, i, 0], qbuf.at[a, i, 1], q_fwd.at[a, i], q_recv.at[a, i, 1], ctx=sib
        )

    def q_start(a):
        q_sib(a).start()
        loop(1, chips, lambda i: q_direct(a, i).start())

    q_start(0)
    qbuf[0, 0, 0] = q_ref[:hrows, :]
    qbuf[1, 0, 0] = q_ref[hrows:, :]

    def h_copy(k):
        return remote(hbuf.at[z], hbuf.at[z], h_send.at[k], h_recv.at[k], head=(z + k) % nhead)

    def h_in(k):
        return remote(
            hbuf.at[(z - k + nhead) % nhead], hbuf.at[(z - k + nhead) % nhead],
            h_send.at[k], h_recv.at[k], head=(z + k) % nhead,
        )

    own_rows = pl.ds(pl.multiple_of(c * rows, rows), rows)

    one_hot = jnp.where(
        lax.broadcasted_iota(jnp.int32, (wide, LANES), 1) == 0, 1.0, 0.0
    ).astype(BF16)

    def scores(a, i, j, n):
        block = jnp.concatenate(
            [
                qbuf[a, i, j, :, (n * group + g) * LANES : (n * group + g + 1) * LANES]
                for g in range(group)
            ],
            axis=0,
        )
        return dot(k_ref[n], jnp.concatenate([block, one_hot], axis=1), ((1,), (1,)))

    def weigh(score, a, i, n, out, out_ml):
        top = jnp.max(score, axis=0, keepdims=True)
        prob = jnp.exp2((score - top) * unit).astype(BF16)
        acc = dot(vt_ref[n], prob)
        tot = acc[LANES : LANES + 1, :]
        out[a, i, n * LANES : (n + 1) * LANES, :] = (acc[:LANES, :] / tot).astype(BF16)
        out_ml[a, i, 0, n : n + 1, :] = top
        out_ml[a, i, 1, n : n + 1, :] = tot

    def p_copy(a, i):
        return (
            remote(part.at[a, i], sib_a.at[a, i], p_send.at[a, i, 0], p_recv.at[a, i, 0], ctx=sib),
            remote(
                part_ml.at[a, i], sib_ml.at[a, i], p_send.at[a, i, 1], p_recv.at[a, i, 1], ctx=sib
            ),
        )

    def m_copy(a, i):
        return (
            remote(
                merged.at[a, i], recv_a.at[a, i], m_send.at[a, i, 0], m_recv.at[a, i, 0],
                ctx=peer(i),
            ),
            remote(
                merged_ml.at[a, i], recv_ml.at[a, i], m_send.at[a, i, 1], m_recv.at[a, i, 1],
                ctx=peer(i),
            ),
        )

    def merge(a, i):
        for copy in p_copy(a, i):
            copy.wait_recv()
        m0, l0 = mine_ml[a, i, 0, :kv, :], mine_ml[a, i, 1, :kv, :]
        m1, l1 = sib_ml[a, i, 0, :kv, :], sib_ml[a, i, 1, :kv, :]
        top = jnp.maximum(m0, m1)
        w0 = l0 * jnp.exp2((m0 - top) * unit)
        w1 = l1 * jnp.exp2((m1 - top) * unit)
        tot = w0 + w1
        merged_ml[a, i, 0, :kv, :] = top
        merged_ml[a, i, 1, :kv, :] = tot
        f0, f1 = w0 / tot, w1 / tot
        for n in range(kv):
            cut = slice(n * LANES, (n + 1) * LANES)
            merged[a, i, cut, :] = (
                mine[a, i, cut, :].astype(F32) * f0[n : n + 1, :]
                + sib_a[a, i, cut, :].astype(F32) * f1[n : n + 1, :]
            ).astype(BF16)

        @pl.when(i > 0)
        def _():
            for copy in m_copy(a, i):
                copy.start()

    def z_copy(a, k):
        return remote(
            z_out.at[a, k], z_in.at[a, k], z_send.at[a, k], z_recv.at[a, k], head=(z + k) % nhead
        )

    def combine(a):
        tops = [merged_ml[a, 0, 0, :kv, :]] + [recv_ml[a, i, 0, :kv, :] for i in range(1, chips)]
        tots = [merged_ml[a, 0, 1, :kv, :]] + [recv_ml[a, i, 1, :kv, :] for i in range(1, chips)]
        top = functools.reduce(jnp.maximum, tops)
        weights = [t * jnp.exp2((m - top) * unit) for m, t in zip(tops, tots)]
        whole = functools.reduce(jnp.add, weights)
        weights = [w / whole for w in weights]
        for n in range(kv):
            cut = slice(n * LANES, (n + 1) * LANES)
            acc = merged[a, 0, cut, :].astype(F32) * weights[0][n : n + 1, :]
            for i in range(1, chips):
                acc = acc + recv_a[a, i, cut, :].astype(F32) * weights[i][n : n + 1, :]
            turned = acc.T.astype(BF16)
            for g in range(group):
                h = n * group + g
                attn[a, :, h * LANES : (h + 1) * LANES] = turned[g * hrows : (g + 1) * hrows, :]

        def project(owner):
            cols = pl.ds(pl.multiple_of(owner * width, width), width)
            return dot(attn[a], op[:, cols])

        def z_step(k):
            z_out[a, k] = project((z + k) % nhead).astype(BF16)
            z_copy(a, k).start()

        loop(1, nhead, z_step)
        own_z[a] = project(z)

    def partials_in(a):
        def wait(i):
            for copy in m_copy(a, i):
                copy.wait_recv()

        loop(1, chips, wait)

    def chip_step(a, i):
        @pl.when(i > 0)
        def _():
            q_direct(a, i).wait_recv()
            q_forward(a, i).start()

        todo = [(0, n) for n in range(kv)] + [(1, n) for n in range(kv)]
        ahead = scores(a, i, *todo[0])
        for at, (j, n) in enumerate(todo):
            score = ahead
            if at + 1 < len(todo):
                if at + 1 == kv:
                    q_forward(a, i).wait_recv()
                ahead = scores(a, i, *todo[at + 1])
            weigh(score, a, i, n, *((part, part_ml) if j else (mine, mine_ml)))
        for copy in p_copy(a, i):
            copy.start()

        if a == 0:
            @pl.when(i > 0)
            def _():
                merge(0, i - 1)

            @pl.when(i == 1)
            def _():
                q_start(1)
        else:
            @pl.when(i == 0)
            def _():
                merge(0, chips - 1)

            @pl.when(i > 0)
            def _():
                merge(1, i - 1)

            @pl.when(i == chips // 2)
            def _():
                partials_in(0)
                load_op.wait()
                combine(0)

    loop(0, chips, lambda i: chip_step(0, i))

    hbuf[z] = dot(st_ref[...], ai_ref[...])
    loop(1, nhead, lambda k: h_copy(k).start())
    st_all[own_rows, :] = st_ref[...]

    loop(0, chips, lambda i: chip_step(1, i))
    merge(1, chips - 1)

    loop(1, nhead, lambda k: h_in(k).wait_recv())
    hidden = hbuf[0]
    for k in range(1, nhead):
        hidden = hidden + hbuf[k]
    sig = jax.nn.sigmoid(hidden)
    active32 = (hidden * sig).astype(BF16).astype(F32)
    active = active32.astype(BF16)
    active_t = active32.T.astype(BF16)

    partials_in(1)

    def s_direct(i):
        return remote(st_ref, st_all.at[own_rows], s_send.at[i], s_recv.at[i, 0], ctx=peer(i))

    def s_sib():
        return remote(st_ref, st_all.at[own_rows], s_send.at[0], s_recv.at[0, 1], ctx=sib)

    def s_forward(i):
        its = pl.ds(pl.multiple_of(peer(i) * rows, rows), rows)
        return remote(st_all.at[its], st_all.at[its], s_fwd.at[i], s_recv.at[i, 1], ctx=sib)

    def s_in(i):
        its = pl.ds(pl.multiple_of(peer(i) * rows, rows), rows)
        return remote(st_ref, st_all.at[its], s_send.at[i], s_recv.at[i, 0], ctx=peer(i))

    def s_in_sib(i):
        owner = peer(i) + 1 - 2 * par
        its = pl.ds(pl.multiple_of(owner * rows, rows), rows)
        return remote(st_ref, st_all.at[its], s_send.at[i], s_recv.at[i, 1], ctx=sib)

    s_sib().start()
    loop(1, chips, lambda i: s_direct(i).start())

    combine(1)
    student = dot(active, ao_ref[...])

    def s_relay(i):
        s_in(i).wait_recv()
        s_forward(i).start()

    loop(1, chips, s_relay)
    for a in range(2):
        loop(1, nhead, lambda k: z_copy(a, k).wait_recv())
        own = own_z[a]
        for k in range(1, nhead):
            own = own + z_in[a, k].astype(F32)
        teacher_ref[a * hrows : (a + 1) * hrows, :] = own.astype(BF16)
    diff = student - teacher_ref[...].astype(F32)
    cotan = (diff * (1.0 / math.sqrt(total_rows))).astype(BF16)

    bbuf[z] = dot(cotan, ao_ref[...], ((1,), (1,))).astype(BF16)
    square = diff * diff
    lane = square[:, :LANES]
    for n in range(1, width // LANES):
        lane = lane + square[:, n * LANES : (n + 1) * LANES]
    lbuf[z] = jnp.sum(lane.reshape(rows // 8, 8, LANES), axis=0)

    def b_copy(k):
        to = (z + k) % nhead
        return (
            remote(bbuf.at[z], bbuf.at[z], b_send.at[k, 0], b_recv.at[k, 0], head=to),
            remote(lbuf.at[z], lbuf.at[z], b_send.at[k, 1], b_recv.at[k, 1], head=to),
        )

    def b_in(k):
        src = (z - k + nhead) % nhead
        return (
            remote(bbuf.at[src], bbuf.at[src], b_send.at[k, 0], b_recv.at[k, 0], head=src),
            remote(lbuf.at[src], lbuf.at[src], b_send.at[k, 1], b_recv.at[k, 1], head=src),
        )

    def b_start(k):
        for copy in b_copy(k):
            copy.start()

    loop(1, nhead, b_start)

    cw = width * (gpart.shape[0] // CHUNK_ROWS) // nctx
    ncol = width // cw

    def chunk(ref, d):
        return ref.at[
            pl.ds(pl.multiple_of((d // ncol) * CHUNK_ROWS, CHUNK_ROWS), CHUNK_ROWS),
            pl.ds(pl.multiple_of((d % ncol) * cw, cw), cw),
        ]

    gpart[...] = dot(active_t, cotan).astype(BF16)

    def r_copy(k):
        d = (c + k) % nctx
        return remote(chunk(gpart, d), gred.at[c], r_send.at[k], r_recv.at[k], ctx=d)

    def r_in(k):
        src = (c - k + nctx) % nctx
        return remote(chunk(gpart, c), gred.at[src], r_send.at[k], r_recv.at[k], ctx=src)

    loop(1, nctx, lambda k: r_copy(k).start())
    gred[c] = chunk(gpart, c)[...]

    def b_wait(k):
        for copy in b_in(k):
            copy.wait_recv()

    loop(1, nhead, b_wait)
    back, squares = bbuf[0].astype(F32), lbuf[0]
    for k in range(1, nhead):
        back = back + bbuf[k].astype(F32)
        squares = squares + lbuf[k]
    g_all[own_rows, :] = (
        back * sig * (1.0 + hidden * (1.0 - sig))
    ).astype(BF16)
    l_all[c] = squares

    def g_copy(k):
        d = (c + k) % nctx
        return (
            remote(g_all.at[own_rows], g_all.at[own_rows], g_send.at[k], g_recv.at[k], ctx=d),
            remote(l_all.at[c], l_all.at[c], l_send.at[k], l_recv.at[k], ctx=d),
        )

    def g_in(k):
        src = (c - k + nctx) % nctx
        its = pl.ds(pl.multiple_of(src * rows, rows), rows)
        return (
            remote(g_all.at[its], g_all.at[its], g_send.at[k], g_recv.at[k], ctx=src),
            remote(l_all.at[src], l_all.at[src], l_send.at[k], l_recv.at[k], ctx=src),
        )

    def g_start(k):
        for copy in g_copy(k):
            copy.start()

    loop(1, nctx, g_start)

    loop(1, nctx, lambda k: r_in(k).wait_recv())
    total = gred[0].astype(F32)
    for k in range(1, nctx):
        total = total + gred[k].astype(F32)
    chunk(gfull, c)[...] = total.astype(BF16)

    def a_copy(k):
        d = (c + k) % nctx
        return remote(chunk(gfull, c), chunk(gfull, c), a_send.at[k], a_recv.at[k], ctx=d)

    def a_in(k):
        src = (c - k + nctx) % nctx
        return remote(chunk(gfull, src), chunk(gfull, src), a_send.at[k], a_recv.at[k], ctx=src)

    loop(1, nctx, lambda k: a_copy(k).start())

    loop(0, chips, lambda i: s_in_sib(i).wait_recv())

    def g_wait(k):
        for copy in g_in(k):
            copy.wait_recv()

    loop(1, nctx, g_wait)
    inner_t = g_all[...].astype(F32).T.astype(BF16)
    gi_ref[...] = dot(inner_t, st_all[...])
    squares = l_all[0]
    for k in range(1, nctx):
        squares = squares + l_all[k]
    loss = jnp.sum(jnp.sum(squares, axis=0, keepdims=True), axis=1, keepdims=True)
    loss_ref[...] = loss / (total_rows * total_width)

    loop(1, nctx, lambda k: a_in(k).wait_recv())
    go_ref[...] = gfull[...]

    s_sib().wait_send()
    for a in range(2):
        q_sib(a).wait_send()

        def p_sent(i):
            for copy in p_copy(a, i):
                copy.wait_send()

        loop(0, chips, p_sent)

        def chips_sent(i):
            q_direct(a, i).wait_send()
            q_forward(a, i).wait_send()
            for copy in m_copy(a, i):
                copy.wait_send()

        loop(1, chips, chips_sent)
        loop(1, nhead, lambda k: z_copy(a, k).wait_send())

    def states_sent(i):
        s_direct(i).wait_send()
        s_forward(i).wait_send()

    loop(1, chips, states_sent)

    def head_sent(k):
        h_copy(k).wait_send()
        for copy in b_copy(k):
            copy.wait_send()

    loop(1, nhead, head_sent)

    def ctx_sent(k):
        r_copy(k).wait_send()
        a_copy(k).wait_send()
        for copy in g_copy(k):
            copy.wait_send()

    loop(1, nctx, ctx_sent)


def shards(queries, cache_keys, cache_values, shard_len, out_proj, states, adapter_in, adapter_out):
    nctx, nhead = lax.axis_size("ctx"), lax.axis_size("head")
    rows, width = queries.shape
    length, kv, hd = cache_keys.shape
    rank = adapter_in.shape[1]
    chips = nctx // 2
    unit = hd ** (-0.5) * math.log2(math.e)
    live = jnp.arange(length, dtype=jnp.int32) < shard_len[0]
    bias = jnp.where(live, 0.0, -1e30).astype(BF16)
    first = jnp.arange(hd) == 0
    keys = jnp.transpose(cache_keys, (1, 0, 2))
    extra = jnp.where(first[None, :], bias[:, None], jnp.zeros((), BF16))
    keys = jnp.concatenate([keys, jnp.broadcast_to(extra[None], keys.shape)], axis=2)
    vals = jnp.transpose(cache_values, (1, 2, 0))
    vals = jnp.concatenate([vals, jnp.ones((kv, CHUNK_ROWS, length), BF16)], axis=1)
    hrows = rows // 2
    wide = width // LANES // kv * hrows
    dma = pltpu.SemaphoreType.DMA
    vmem = pl.BlockSpec(memory_space=pltpu.VMEM)
    cw = width * (rank // CHUNK_ROWS) // nctx
    blocks = [
        pltpu.VMEM((2, chips, kv * LANES, wide), BF16),
        pltpu.VMEM((2, chips, 2, 8, wide), F32),
    ]
    scratch = [
        pltpu.VMEM(out_proj.shape, BF16),
        pltpu.VMEM((2, chips, 2, hrows, width), BF16),
        *(blocks * 5),
        pltpu.VMEM((2, hrows, width), BF16),
        pltpu.VMEM((2, hrows, width), F32),
        pltpu.VMEM((2, nhead, hrows, width), BF16),
        pltpu.VMEM((2, nhead, hrows, width), BF16),
        pltpu.VMEM((nhead, rows, rank), F32),
        pltpu.VMEM((nhead, rows, rank), BF16),
        pltpu.VMEM((nhead, 8, LANES), F32),
        pltpu.VMEM((nctx * rows, width), BF16),
        pltpu.VMEM((nctx * rows, rank), BF16),
        pltpu.VMEM((nctx, 8, LANES), F32),
        pltpu.VMEM((rank, width), BF16),
        pltpu.VMEM((nctx, CHUNK_ROWS, cw), BF16),
        pltpu.VMEM((rank, width), BF16),
        dma,
        dma((2, chips)), dma((2, chips)), dma((2, chips, 2)),
        dma((2, chips, 2)), dma((2, chips, 2)),
        dma((2, chips, 2)), dma((2, chips, 2)),
        dma((2, nhead)), dma((2, nhead)),
        dma((nhead,)), dma((nhead,)),
        dma((nhead, 2)), dma((nhead, 2)),
        dma((chips,)), dma((chips,)), dma((chips, 2)),
        dma((nctx,)), dma((nctx,)), dma((nctx,)), dma((nctx,)),
        dma((nctx,)), dma((nctx,)), dma((nctx,)), dma((nctx,)),
    ]
    teacher, loss, grad_in, grad_out = pl.pallas_call(
        functools.partial(
            kernel, nctx, nhead, kv, unit, rows * nctx, width * nhead
        ),
        out_shape=(
            jax.ShapeDtypeStruct((rows, width), BF16),
            jax.ShapeDtypeStruct((1, 1), F32),
            jax.ShapeDtypeStruct((rank, width), F32),
            jax.ShapeDtypeStruct((rank, width), BF16),
        ),
        in_specs=[vmem, vmem, vmem, pl.BlockSpec(memory_space=pl.ANY), vmem, vmem, vmem],
        out_specs=(vmem, vmem, vmem, vmem),
        scratch_shapes=scratch,
        compiler_params=pltpu.CompilerParams(
            collective_id=0, has_side_effects=True, vmem_limit_bytes=50 * 2**20
        ),
    )(queries, keys, vals, out_proj, states, adapter_in, adapter_out)
    return (teacher, loss.reshape(()), grad_in.T, grad_out.astype(F32))


def solution(mesh):
    placed = (
        P("ctx", "head"),
        P("ctx", "head", None),
        P("ctx", "head", None),
        P("ctx"),
        P("head", None),
        P("ctx", "head"),
        P("head", None),
        P(None, "head"),
    )
    return jax.shard_map(
        shards,
        mesh=mesh,
        in_specs=placed,
        out_specs=(P("ctx", "head"), P(), P("head", None), P(None, "head")),
        check_vma=False,
    )
```

time: 92 us -> 76.6 us (0.83)
  Pallas kernels: 83.9 us -> 68.3 us
    pallas_call x1, Pallas kernels: 83.9 us -> 68.3 us  [shards(): pl.pallas_call(functools.partial(kernel, nctx, nhead, kv, unit, rows * nc...]
    unnamed x15 -> x14, local copies, waits for them, and re-layouts: 4.38 us -> 3.78 us
where the time goes in v2:
time: 76.6 us; the launch traced here: 76.4 us
  Pallas kernels  68.3 us (89%)
  local copies, waits for them, and re-layouts  3.87 us (5%)
  between operations  3.08 us (4%)
  other arithmetic  1.17 us (2%)
    pallas_call x1, Pallas kernels, shards(): pl.pallas_call(functools.partial(kernel, nctx, nhead, kv, unit, rows * nc...  68.3 us
    unnamed x14, local copies, waits for them, and re-layouts  3.78 us

profile of v2, /device:TPU:0, one launch (start us, length us, event | category | flops | bytes accessed | tf_op | source)
XLA Modules:
  0.0 76.4 jit_solution(14146277293642227406)
XLA Ops:
  1.3 0.0 copy-start.4
  1.3 0.2 broadcast_select_fusion
  1.6 1.1 %copy.16 = bf16[1024,2,128]{2,0,1:T(8,128)(2,1)S(1)} copy(bf16[1024,2,128]{2,1,0:T(2,128)(2,1)} %param.9) | data formatting | bytes 1048576 | tf_op args[1]
  2.7 0.0 copy-start
  2.7 0.0 copy-start.1
  2.7 0.0 copy-start.2
  2.7 0.0 copy-start.3
  2.7 0.1 pad_maximum_fusion.k_ref
  2.9 0.0 copy-done.4
  2.9 0.4 copy.13
  3.3 0.3 copy-done
  3.6 0.1 copy-done.1
  3.7 0.1 copy-done.2
  3.8 0.1 copy-done.3
  3.9 68.3 %shard_map.111 = (bf16[128,1024]{1,0:T(8,128)(2,1)S(1)}, f32[1,1]{1,0:T(1,128)}, f32[128,1024]{1,0:T(8,128)S(1)}, bf16[128,1024]{1,0:T(8,128)(2,1)S(1)}) custom-call(bf16[128,1024]{1,0:T(8,128)(2,1)S(1)} %copy-done, bf16[2,1024,256]{2,1,0:T(8,128)(2,1)S(1)} %pad_maximum_fusion.k_ref, bf16[2,144,1024]{2,1,0:T(8,128)(2,1)S(1)} %concatenate.7.vt_ref, ...), custom_call_target="tpu_custom_call" | custom-call | tf_op jit(solution)/shard_map/pallas_call | solution.py:540
  72.2 1.0 %copy.14 = f32[1024,128]{1,0:T(8,128)} copy(f32[1024,128]{0,1:T(8,128)S(1)} %bitcast.8) | data formatting | bytes 1048576
  73.2 0.8 %convert_element_type.11 = f32[128,1024]{1,0:T(8,128)} convert(bf16[128,1024]{1,0:T(8,128)(2,1)S(1)} %get-tuple-element.11) | non-fusion elementwise | flops 131072 | bytes 786432 | tf_op jit(solution)/shard_map/convert_element_type | solution.py:557
  74.0 0.7 copy.20
  (4 shorter events, 0.1 us)
Async XLA Ops:
  1.3 1.6 %copy-start.4 = (bf16[1024,2,128]{2,1,0:T(2,128)(2,1)S(1)}, bf16[1024,2,128]{2,1,0:T(2,128)(2,1)}, u32[]{:S(2)}) copy-start(bf16[1024,2,128]{2,1,0:T(2,128)(2,1)} %param.10) | copy-start | bytes 1572868
  2.7 1.0 %copy-start = (bf16[128,1024]{1,0:T(8,128)(2,1)S(1)}, bf16[128,1024]{1,0:T(8,128)(2,1)}, u32[]{:S(2)}) copy-start(bf16[128,1024]{1,0:T(8,128)(2,1)} %q_ref.1) | copy-start | bytes 786436
  2.7 1.0 %copy-start.1 = (bf16[128,1024]{1,0:T(8,128)(2,1)S(1)}, bf16[128,1024]{1,0:T(8,128)(2,1)}, u32[]{:S(2)}) copy-start(bf16[128,1024]{1,0:T(8,128)(2,1)} %st_ref.1) | copy-start | bytes 786436
  2.7 1.1 %copy-start.2 = (bf16[1024,128]{1,0:T(8,128)(2,1)S(1)}, bf16[1024,128]{1,0:T(8,128)(2,1)}, u32[]{:S(2)}) copy-start(bf16[1024,128]{1,0:T(8,128)(2,1)} %ai_ref.1) | copy-start | bytes 786436
  2.7 1.2 %copy-start.3 = (bf16[128,1024]{1,0:T(8,128)(2,1)S(1)}, bf16[128,1024]{1,0:T(8,128)(2,1)}, u32[]{:S(2)}) copy-start(bf16[128,1024]{1,0:T(8,128)(2,1)} %ao_ref.1) | copy-start | bytes 786436

commit v3 on v2

--- a/solution.py
+++ b/solution.py
@@ -249,19 +249,19 @@
             def _():
                 merge(0, i - 1)
 
-            @pl.when(i == 1)
+            @pl.when(i == 0)
             def _():
                 q_start(1)
         else:
-            @pl.when(i == 0)
+            @pl.when(i == chips - 1)
             def _():
                 merge(0, chips - 1)
 
-            @pl.when(i > 0)
+            @pl.when(i < chips - 1)
             def _():
-                merge(1, i - 1)
-
-            @pl.when(i == chips // 2)
+                merge(1, i + 1)
+
+            @pl.when(i == chips // 2 - 1)
             def _():
                 partials_in(0)
                 load_op.wait()
@@ -273,8 +273,8 @@
     loop(1, nhead, lambda k: h_copy(k).start())
     st_all[own_rows, :] = st_ref[...]
 
-    loop(0, chips, lambda i: chip_step(1, i))
-    merge(1, chips - 1)
+    loop(0, chips, lambda t: chip_step(1, chips - 1 - t))
+    merge(1, 0)
 
     loop(1, nhead, lambda k: h_in(k).wait_recv())
     hidden = hbuf[0]

time: 76.6 us -> 74.9 us (0.978)
  Pallas kernels: 68.3 us -> 66.6 us
    pallas_call x1, Pallas kernels: 68.3 us -> 66.6 us  [shards(): pl.pallas_call(functools.partial(kernel, nctx, nhead, kv, unit, rows * nc...]
where the time goes in v3:
time: 74.9 us; the launch traced here: 74.7 us
  Pallas kernels  66.6 us (89%)
  local copies, waits for them, and re-layouts  3.87 us (5%)
  between operations  3.08 us (4%)
  other arithmetic  1.17 us (2%)
    pallas_call x1, Pallas kernels, shards(): pl.pallas_call(functools.partial(kernel, nctx, nhead, kv, unit, rows * nc...  66.6 us
    unnamed x14, local copies, waits for them, and re-layouts  3.78 us

profile of v3, /device:TPU:0, one launch (start us, length us, event | category | flops | bytes accessed | tf_op | source)
XLA Modules:
  0.0 74.7 jit_solution(1419060721167774448)
XLA Ops:
  1.3 0.0 copy-start.4
  1.3 0.2 broadcast_select_fusion
  1.6 1.1 %copy.16 = bf16[1024,2,128]{2,0,1:T(8,128)(2,1)S(1)} copy(bf16[1024,2,128]{2,1,0:T(2,128)(2,1)} %param.9) | data formatting | bytes 1048576 | tf_op args[1]
  2.7 0.0 copy-start
  2.7 0.0 copy-start.1
  2.7 0.0 copy-start.2
  2.7 0.0 copy-start.3
  2.7 0.1 pad_maximum_fusion.k_ref
  2.9 0.0 copy-done.4
  2.9 0.4 copy.13
  3.3 0.3 copy-done
  3.6 0.1 copy-done.1
  3.7 0.1 copy-done.2
  3.8 0.1 copy-done.3
  3.9 66.6 %shard_map.111 = (bf16[128,1024]{1,0:T(8,128)(2,1)S(1)}, f32[1,1]{1,0:T(1,128)}, f32[128,1024]{1,0:T(8,128)S(1)}, bf16[128,1024]{1,0:T(8,128)(2,1)S(1)}) custom-call(bf16[128,1024]{1,0:T(8,128)(2,1)S(1)} %copy-done, bf16[2,1024,256]{2,1,0:T(8,128)(2,1)S(1)} %pad_maximum_fusion.k_ref, bf16[2,144,1024]{2,1,0:T(8,128)(2,1)S(1)} %concatenate.7.vt_ref, ...), custom_call_target="tpu_custom_call" | custom-call | tf_op jit(solution)/shard_map/pallas_call | solution.py:540
  70.5 1.0 %copy.14 = f32[1024,128]{1,0:T(8,128)} copy(f32[1024,128]{0,1:T(8,128)S(1)} %bitcast.8) | data formatting | bytes 1048576
  71.5 0.8 %convert_element_type.11 = f32[128,1024]{1,0:T(8,128)} convert(bf16[128,1024]{1,0:T(8,128)(2,1)S(1)} %get-tuple-element.11) | non-fusion elementwise | flops 131072 | bytes 786432 | tf_op jit(solution)/shard_map/convert_element_type | solution.py:557
  72.3 0.7 copy.20
  (4 shorter events, 0.1 us)
Async XLA Ops:
  1.3 1.6 %copy-start.4 = (bf16[1024,2,128]{2,1,0:T(2,128)(2,1)S(1)}, bf16[1024,2,128]{2,1,0:T(2,128)(2,1)}, u32[]{:S(2)}) copy-start(bf16[1024,2,128]{2,1,0:T(2,128)(2,1)} %param.10) | copy-start | bytes 1572868
  2.7 1.0 %copy-start = (bf16[128,1024]{1,0:T(8,128)(2,1)S(1)}, bf16[128,1024]{1,0:T(8,128)(2,1)}, u32[]{:S(2)}) copy-start(bf16[128,1024]{1,0:T(8,128)(2,1)} %q_ref.1) | copy-start | bytes 786436
  2.7 1.0 %copy-start.1 = (bf16[128,1024]{1,0:T(8,128)(2,1)S(1)}, bf16[128,1024]{1,0:T(8,128)(2,1)}, u32[]{:S(2)}) copy-start(bf16[128,1024]{1,0:T(8,128)(2,1)} %st_ref.1) | copy-start | bytes 786436
  2.7 1.1 %copy-start.2 = (bf16[1024,128]{1,0:T(8,128)(2,1)S(1)}, bf16[1024,128]{1,0:T(8,128)(2,1)}, u32[]{:S(2)}) copy-start(bf16[1024,128]{1,0:T(8,128)(2,1)} %ai_ref.1) | copy-start | bytes 786436
  2.7 1.2 %copy-start.3 = (bf16[128,1024]{1,0:T(8,128)(2,1)S(1)}, bf16[128,1024]{1,0:T(8,128)(2,1)}, u32[]{:S(2)}) copy-start(bf16[128,1024]{1,0:T(8,128)(2,1)} %ao_ref.1) | copy-start | bytes 786436
